TPU v7x, 32 devices: a whole 2x2x4 slice. The times are simulated.
32 devices in a mesh: ctx: 8 (over z, y), ch: 4 (over x, core).
Axes of the slice: x: 2, y: 2, z: 4, core: 2. Of those that a mesh axis runs over, the one named last changes fastest.
Arguments:
- conv_input: bfloat16 [32, 128, 8192], P('ctx', None, 'ch'), may hold values from -6 to 6
- gate_signal: bfloat16 [32, 128, 8192], P('ctx', None, 'ch'), may hold values from -6 to 6
- cotangent: bfloat16 [32, 128, 8192], P('ctx', None, 'ch'), may hold values from -6 to 6
- filters: float32 [16, 1024], replicated
- tile_owner: int32 [24], replicated, may hold values from 0 to 7, as said below
- support: int32 [24, 8], replicated, may hold values from -1 to 23, as said below
Outputs:
- gate_grad: bfloat16 [32, 128, 8192], P('ctx', None, 'ch')
- input_grad: bfloat16 [32, 128, 8192], P('ctx', None, 'ch')
- filter_grad: float32 [16, 1024], replicated
Inputs may be any that keep to these rules, and one draw needn't show every extreme that they name: tile_owner never falls from one tile to the next; every index of ctx owns from 2 to 4 tiles, some index owns 3 + 1 and some index owns 3 - 1. support[t, k] is t - k where tile t - k belongs to the document of tile t and -1 otherwise; documents are runs of whole tiles, and some document spans 8 tiles or more.
All inputs are finite; a program needn't handle non-finite values.
Results may differ from a plain program's by a relative error of at most 0.0058.
Values may be sent and summed in bfloat16 or wider, within the bound.
A program may use at most 256 MiB of HBM per device.

v0:
```python
import math

import jax
import jax.numpy as jnp
from jax import lax
from jax.sharding import PartitionSpec as P

GROUP = 128
REACH = 4


def passed_along(value, axis, steps):
    count = lax.axis_size(axis)
    leading, last = (max(0, -steps), min(count, count - steps))
    return lax.ppermute(value, axis, [(source, source + steps) for source in range(leading, last)])


def filter_blocks(filters, tile_rows, maxlag):
    narrow = filters.astype(jnp.bfloat16)
    row_ids = jnp.arange(tile_rows, dtype=jnp.int32)
    lag_offsets = (
        jnp.arange(maxlag, dtype=jnp.int32)[:, None, None] * tile_rows
        + row_ids[:, None]
        - row_ids[None, :]
    )
    picked = jnp.take(narrow, jnp.clip(lag_offsets, 0, filters.shape[1] - 1), axis=1)
    return jnp.where(lag_offsets[None] >= 0, picked, jnp.zeros_like(picked))


def lag_sums(square):
    filter_count, side_length = (square.shape[0], square.shape[1])
    flipped = square[:, :, ::-1]
    padded = jnp.pad(flipped, ((0, 0), (0, 0), (0, side_length)))
    skewed = padded.reshape(filter_count, 2 * side_length * side_length)[
        :, : side_length * (2 * side_length - 1)
    ]
    return jnp.sum(skewed.reshape(filter_count, side_length, 2 * side_length - 1), axis=1)


def spread_lags(squares, lag_count):
    maxlag, filter_count, side_length = (squares.shape[0], squares.shape[1], squares.shape[2])
    accumulated = jnp.zeros((filter_count, (maxlag + 1) * side_length), jnp.float32)
    for lag_index in range(maxlag):
        start_col = lag_index * side_length
        accumulated = accumulated.at[:, start_col : start_col + 2 * side_length - 1].add(
            lag_sums(squares[lag_index])
        )
    return accumulated[:, side_length - 1 : side_length - 1 + lag_count]


def per_device(conv_input, gate_signal, cotangent, filters, tile_owner, support):
    slot_count, tile_rows, channels = conv_input.shape
    maxlag = support.shape[1]
    filter_count, lag_count = filters.shape
    group_width = GROUP
    repeats = channels // (filter_count * group_width)
    total_tiles = tile_owner.shape[0]
    devices_ctx = lax.axis_size("ctx")
    myself = lax.axis_index("ctx")
    farthest = REACH
    devices = jnp.arange(devices_ctx, dtype=jnp.int32)
    counts = jnp.sum((tile_owner[None, :] == devices[:, None]).astype(jnp.int32), axis=1)
    starts = jnp.cumsum(counts) - counts
    slot_index = jnp.arange(slot_count, dtype=jnp.int32)
    own_tiles = starts[myself] + slot_index
    own_live = slot_index < counts[myself]
    own_safe = jnp.clip(own_tiles, 0, total_tiles - 1)
    sources = support[own_safe]
    present = own_live[:, None] & (sources >= 0)
    source_safe = jnp.clip(sources, 0, total_tiles - 1)
    holder = tile_owner[source_safe]
    within = source_safe - starts[holder]
    blocks = filter_blocks(filters, tile_rows, maxlag)
    zero_tile = jnp.zeros((), jnp.bfloat16)
    gathered = [conv_input]
    for distance in range(1, farthest + 1):
        gathered.append(passed_along(conv_input, "ctx", distance))
    window = jnp.concatenate(gathered, axis=0)
    rows_at = jnp.clip((myself - holder) * slot_count + within, 0, window.shape[0] - 1)
    selected = jnp.take(window, rows_at.reshape(-1), axis=0)
    selected = selected.reshape(slot_count, maxlag, tile_rows, channels)
    selected = jnp.where(present[:, :, None, None], selected, zero_tile)
    weighted = (gate_signal.astype(jnp.float32) * cotangent.astype(jnp.float32)).astype(
        jnp.bfloat16
    )
    weighted = jnp.where(own_live[:, None, None], weighted, zero_tile)
    weighted_shaped = weighted.reshape(slot_count, tile_rows, repeats, filter_count, group_width)
    conv_out = jnp.zeros((slot_count, tile_rows, channels), jnp.float32)
    squares = []
    for lag_index in range(maxlag):
        shaped = selected[:, lag_index].reshape(
            slot_count, tile_rows, repeats, filter_count, group_width
        )
        product = jnp.einsum(
            "fij,sjrfc->sirfc", blocks[:, lag_index], shaped, preferred_element_type=jnp.float32
        )
        conv_out = conv_out + product.reshape(slot_count, tile_rows, channels)
        squares.append(
            jnp.einsum(
                "sirfc,sjrfc->fij", weighted_shaped, shaped, preferred_element_type=jnp.float32
            )
        )
    gate_grad = (cotangent.astype(jnp.float32) * conv_out).astype(jnp.bfloat16)
    norm_factor = 1.0 / math.sqrt(
        total_tiles * tile_rows * channels * lax.axis_size("ch") / filter_count
    )
    local_filters = spread_lags(jnp.stack(squares), lag_count)
    filter_grad = lax.psum(local_filters, ("ctx", "ch")) * norm_factor
    row_count = (farthest + 1) * slot_count
    partial_value = jnp.zeros((row_count, tile_rows, channels), jnp.float32)
    back_rows = jnp.clip((myself - holder) * slot_count + within, 0, row_count - 1)
    for lag_index in range(maxlag):
        adjoint_term = jnp.einsum(
            "fji,sjrfc->sirfc",
            blocks[:, lag_index],
            weighted_shaped,
            preferred_element_type=jnp.float32,
        )
        adjoint_term = jnp.where(present[:, lag_index, None, None, None, None], adjoint_term, 0.0)
        partial_value = partial_value.at[back_rows[:, lag_index]].add(
            adjoint_term.reshape(slot_count, tile_rows, channels)
        )
    adjoint = partial_value[:slot_count]
    for distance in range(1, farthest + 1):
        adjoint = adjoint + passed_along(
            partial_value[distance * slot_count : (distance + 1) * slot_count], "ctx", -distance
        )
    input_grad = adjoint.astype(jnp.bfloat16)
    return (gate_grad, input_grad, filter_grad)


def solution(mesh):
    return jax.shard_map(
        per_device,
        mesh=mesh,
        in_specs=(P("ctx", None, "ch"), P("ctx", None, "ch"), P("ctx", None, "ch"), P(), P(), P()),
        out_specs=(P("ctx", None, "ch"), P("ctx", None, "ch"), P()),
        check_vma=False,
    )
```

profile of v0, /device:TPU:12, one launch (start us, length us, event | category | flops | bytes accessed | tf_op | source)
XLA Modules:
  0.0 1275.0 jit_solution(11242388865346379157)
XLA Ops:
  27.4 454.0 %gather_fusion.4 = bf16[131072,16]{1,0:T(8,128)(2,1)} fusion(bf16[16,1024]{0,1:T(8,128)(2,1)S(1)} %copy.160, s32[131072]{0:T(1024)S(1)} %broadcast_clamp_fusion), kind=kCustom, calls=%fused_computation.4 | custom fusion | bytes 8912896 | tf_op jit(solution)/shard_map/jit(_take)/gather | solution.py:26
  481.4 29.2 %copy.162 = bf16[8,128,128,16]{2,1,3,0:T(8,128)(2,1)} copy(bf16[8,128,128,16]{3,2,1,0:T(8,128)(2,1)} %bitcast.209) | data formatting | bytes 8388608 | tf_op jit(solution)/shard_map/jit(_take)/gather | solution.py:26
  513.5 3.9 copy.179
  542.9 5.4 copy.182
  548.3 4.7 copy.184
  553.0 5.4 copy.185
  558.4 4.7 copy.187
  563.1 5.4 copy.188
  568.5 4.7 copy.190
  573.1 5.4 copy.191
  578.5 4.7 copy.193
  583.2 5.4 copy.194
  588.6 4.7 copy.196
  593.2 5.6 copy.197
  598.8 4.7 copy.199
  603.5 5.4 copy.200
  608.9 4.6 copy.202
  613.5 5.4 copy.203
  619.2 9.7 broadcast_in_dim.155
  628.9 9.0 scatter_fusion
  637.8 9.0 scatter_fusion.1
  646.9 9.0 scatter_fusion.2
  655.9 9.1 scatter_fusion.3
  664.9 9.0 scatter_fusion.4
  673.9 9.0 scatter_fusion.5
  682.9 8.9 scatter_fusion.6
  691.8 8.9 scatter_fusion.7
  700.8 12.2 fusion.52
  743.1 11.8 gather_fusion.3
  754.9 8.7 select_select_fusion
  763.6 5.9 fusion.53
  769.5 4.0 copy.159
  773.5 4.5 fusion.28
  779.8 4.0 copy.164
  783.7 4.5 fusion.26
  790.0 4.0 copy.166
  793.9 4.5 fusion.24
  799.2 4.0 copy.174
  803.1 4.4 fusion.16
  811.5 4.3 fusion.18
  815.8 4.0 copy.170
  819.8 4.3 fusion.20
  824.1 3.9 copy.168
  828.0 4.5 fusion.22
  832.5 4.1 copy.176
  836.6 11.8 add_bitcast_fusion
  850.6 9.3 rev.24
  864.1 6.2 reshape.668
  872.6 9.3 rev.25
  886.1 6.2 reshape.670
  894.0 6.0 rev.26
  904.2 6.2 reshape.672
  914.4 5.8 rev.27
  924.4 6.2 reshape.674
  934.7 6.2 rev.28
  945.1 6.2 reshape.676
  955.3 5.8 rev.29
  965.3 6.2 reshape.678
  975.6 6.0 rev.30
  985.7 6.2 reshape.680
  1000.3 6.3 reshape.682
  1023.9 159.4 %all-reduce.11.cloned.1.call-done = f32[16,1024]{1,0:T(8,128)} async-done(((f32[16,1024]{1,0:T(8,128)}), f32[16,1024]{1,0:T(8,128)}) %all-reduce.11.cloned.1.call-update) | async-done | bytes 65552 | tf_op jit(solution)/shard_map/psum | solution.py:108
  1184.7 72.9 %collective-permute-done.4 = f32[4,128,2048]{2,1,0:T(8,128)} collective-permute-done((f32[4,128,2048]{2,1,0:T(8,128)}, f32[4,128,2048]{2,1,0:T(8,128)}, u32[]{:S(2)}, u32[]{:S(2)}) %collective-permute-start.4) | collective-permute-done | bytes 4194336 | tf_op jit(solution)/shard_map/ppermute | solution.py:15
  1257.6 10.4 fusion.5
  (156 shorter events, 165.8 us)
Async XLA Ops:
  7.2 20.0 %copy-start.7 = (f32[16,1024]{1,0:T(8,128)S(1)}, f32[16,1024]{1,0:T(8,128)}, u32[]{:S(2)}) copy-start(f32[16,1024]{1,0:T(8,128)} %param.25) | copy-start | bytes 196612
  7.2 1176.1 %all-reduce.11.cloned.1.call-start = ((), (), s32[]{:S(2)}) async-start(), calls=%async_computation | async-start | bytes 131072 | tf_op jit(solution)/shard_map/psum | solution.py:108
  7.2 715.7 %collective-permute-start = (bf16[4,128,2048]{2,1,0:T(8,128)(2,1)}, bf16[4,128,2048]{2,1,0:T(8,128)(2,1)}, u32[]{:S(2)}, u32[]{:S(2)}) collective-permute-start(bf16[4,128,2048]{2,1,0:T(8,128)(2,1)} %param.22), channel_id=1, source_target_pairs={{0,4},{4,8},{8,12},{12,16},{16,20},{20,24},{24,28},{1,5},{5,9},{9,... | collective-permute-start | bytes 6291464 | tf_op jit(solution)/shard_map/ppermute | solution.py:15
  10.7 717.4 %collective-permute-start.1 = (bf16[4,128,2048]{2,1,0:T(8,128)(2,1)}, bf16[4,128,2048]{2,1,0:T(8,128)(2,1)}, u32[]{:S(2)}, u32[]{:S(2)}) collective-permute-start(bf16[4,128,2048]{2,1,0:T(8,128)(2,1)} %param.22), channel_id=1, source_target_pairs={{0,8},{4,12},{8,16},{12,20},{16,24},{20,28},{1,9},{5,13},{9,17},{1... | collective-permute-start | bytes 6291464 | tf_op jit(solution)/shard_map/ppermute | solution.py:15
  14.2 719.0 %collective-permute-start.2 = (bf16[4,128,2048]{2,1,0:T(8,128)(2,1)}, bf16[4,128,2048]{2,1,0:T(8,128)(2,1)}, u32[]{:S(2)}, u32[]{:S(2)}) collective-permute-start(bf16[4,128,2048]{2,1,0:T(8,128)(2,1)} %param.22), channel_id=1, source_target_pairs={{0,12},{4,16},{8,20},{12,24},{16,28},{1,13},{5,17},{9,21},{13,25},... | collective-permute-start | bytes 6291464 | tf_op jit(solution)/shard_map/ppermute | solution.py:15
  16.4 723.5 %collective-permute-start.3 = (bf16[4,128,2048]{2,1,0:T(8,128)(2,1)}, bf16[4,128,2048]{2,1,0:T(8,128)(2,1)}, u32[]{:S(2)}, u32[]{:S(2)}) collective-permute-start(bf16[4,128,2048]{2,1,0:T(8,128)(2,1)} %param.22), channel_id=1, source_target_pairs={{0,16},{4,20},{8,24},{12,28},{1,17},{5,21},{9,25},{13,29},{2,18},{... | collective-permute-start | bytes 6291464 | tf_op jit(solution)/shard_map/ppermute | solution.py:15
  481.4 29.2 %copy-start.6 = (bf16[4,128,2048]{2,1,0:T(8,128)(2,1)S(1)}, bf16[4,128,2048]{2,1,0:T(8,128)(2,1)}, u32[]{:S(2)}) copy-start(bf16[4,128,2048]{2,1,0:T(8,128)(2,1)} %param.24) | copy-start | bytes 6291460
  517.4 3.4 copy-start.5
  521.3 16.7 %copy-start = (bf16[16,8,128,128]{3,2,0,1:T(8,128)(2,1)}, bf16[16,8,128,128]{3,2,0,1:T(8,128)(2,1)S(1)}, u32[]{:S(2)}) copy-start(bf16[16,8,128,128]{3,2,0,1:T(8,128)(2,1)S(1)} %select_bitcast_fusion) | copy-start | bytes 12582916
  713.0 471.7 %collective-permute-start.7 = (f32[4,128,2048]{2,1,0:T(8,128)}, f32[4,128,2048]{2,1,0:T(8,128)}, u32[]{:S(2)}, u32[]{:S(2)}) collective-permute-start(f32[4,128,2048]{2,1,0:T(8,128)} %get-tuple-element.127), channel_id=1, source_target_pairs={{16,0},{20,4},{24,8},{28,12},{17,1},{21,5},{25,9},{29,13},{18,2},{... | collective-permute-start | bytes 12582920 | tf_op jit(solution)/shard_map/ppermute | solution.py:15
  723.0 461.8 %collective-permute-start.6 = (f32[4,128,2048]{2,1,0:T(8,128)}, f32[4,128,2048]{2,1,0:T(8,128)}, u32[]{:S(2)}, u32[]{:S(2)}) collective-permute-start(f32[4,128,2048]{2,1,0:T(8,128)} %get-tuple-element.128), channel_id=1, source_target_pairs={{12,0},{16,4},{20,8},{24,12},{28,16},{13,1},{17,5},{21,9},{25,13},... | collective-permute-start | bytes 12582920 | tf_op jit(solution)/shard_map/ppermute | solution.py:15
  728.0 456.7 %collective-permute-start.5 = (f32[4,128,2048]{2,1,0:T(8,128)}, f32[4,128,2048]{2,1,0:T(8,128)}, u32[]{:S(2)}, u32[]{:S(2)}) collective-permute-start(f32[4,128,2048]{2,1,0:T(8,128)} %get-tuple-element.129), channel_id=1, source_target_pairs={{8,0},{12,4},{16,8},{20,12},{24,16},{28,20},{9,1},{13,5},{17,9},{2... | collective-permute-start | bytes 12582920 | tf_op jit(solution)/shard_map/ppermute | solution.py:15
  733.2 524.5 %collective-permute-start.4 = (f32[4,128,2048]{2,1,0:T(8,128)}, f32[4,128,2048]{2,1,0:T(8,128)}, u32[]{:S(2)}, u32[]{:S(2)}) collective-permute-start(f32[4,128,2048]{2,1,0:T(8,128)} %get-tuple-element.126), channel_id=1, source_target_pairs={{4,0},{8,4},{12,8},{16,12},{20,16},{24,20},{28,24},{5,1},{9,5},{13... | collective-permute-start | bytes 12582920 | tf_op jit(solution)/shard_map/ppermute | solution.py:15
  773.5 4.5 copy-start.2
  783.7 4.5 copy-start.3
  793.9 4.5 copy-start.4
  1000.3 15.8 %copy-start.1 = (bf16[4,128,2048]{1,2,0:T(8,128)(2,1)S(1)}, bf16[4,128,2048]{1,2,0:T(8,128)(2,1)}, u32[]{:S(2)}) copy-start(bf16[4,128,2048]{1,2,0:T(8,128)(2,1)} %copy.157) | copy-start | bytes 6291460
Sparse Core Ops, SparseCore 0:
  1016.2 167.0 all-reduce.10
where the time goes:
time: 1290 us; the launch traced here: 1280 us
  local copies, waits for them, and re-layouts  801 us (62%)
  waiting for transfers between devices  232 us (18%)
  other arithmetic  128 us (10%)
  matrix products  78 us (6%)
  starting transfers between devices  20.6 us (2%)
  between operations  14.8 us (1%)
    gather x2, local copies, waits for them, and re-layouts, filter_blocks(): jnp.take(narrow, jnp.clip(lag_offsets, 0, filters.shape[1] - 1), axis=1)  483 us
    psum x1, waiting for transfers between devices, per_device(): filter_grad = lax.psum(local_filters, ('ctx', 'ch')) * norm_factor  159 us
    ppermute x8, waiting for transfers between devices, passed_along(): lax.ppermute(value, axis, [(source, source + steps) for source in range(l...  72.9 us
    scatter-add x8, other arithmetic, per_device(): partial_value.at[back_rows[:, lag_index]]  71.9 us
    rev x8, local copies, waits for them, and re-layouts, lag_sums(): flipped = square[:, :, ::-1]  50 us
    reshape x8, local copies, waits for them, and re-layouts, lag_sums(): skewed.reshape(filter_count, side_length, 2 * side_length - 1)  49.4 us
    reshape x8, local copies, waits for them, and re-layouts, per_device(): adjoint_term.reshape(slot_count, tile_rows, channels)  43.4 us
    dot_general x8, matrix products, per_device(): jnp.einsum('fij,sjrfc->sirfc', blocks[:, lag_index], shaped, preferred_el...  42.7 us
  transfers between devices with their start and end apart: 9, of which 2 were waited for; matrix products, arithmetic and copies ran while one was open for 78% of the time, Pallas kernels for 0%

commit v1 on v0

v1 whole, which is shorter than its diff:
```python
import functools
import math

import jax
import jax.numpy as jnp
from jax import lax
from jax.experimental import pallas as pl
from jax.experimental.pallas import tpu as pltpu
from jax.sharding import PartitionSpec as P

GROUP = 128
LEAD = 8
LO = 4
MESH = pl.DeviceIdType.MESH


def copy_to(src, dst, send, recv, ctx):
    return pltpu.make_async_remote_copy(
        src_ref=src,
        dst_ref=dst,
        send_sem=send,
        recv_sem=recv,
        device_id={"ctx": ctx},
        device_id_type=MESH,
    )


def kernel(
    n_ctx,
    tab,
    x_ref,
    gate_ref,
    cot_ref,
    taps_ref,
    rtaps_ref,
    fmask_ref,
    bmask_ref,
    gg_ref,
    ig_ref,
    fg_ref,
    xr,
    wr,
    ws,
    hx,
    gw,
    sx,
    tw,
    rc,
    ra,
    sc,
    sa,
    cx,
    cw,
    mat_a,
    mat_b,
    rhs,
    vv,
    co,
    ao,
    y_send,
    y_recv,
    z_send,
    z_recv,
):
    slots, rows, channels = x_ref.shape
    half = channels // 2
    chunks = half // GROUP
    lags = taps_ref.shape[1]
    own = 2 * slots
    reach = lags - 1
    f32, bf16 = jnp.float32, jnp.bfloat16
    me = lax.axis_index("ctx")
    pair = me // 2
    side = me % 2
    partner = me + 1 - 2 * side
    up, down = me + 2, me - 2
    has_up = pair < n_ctx // 2 - 1
    has_down = pair > 0
    t_s, t_t, t_w, t_v, t_mine, t_theirs = 0, 7, 14, 29, 44, 48

    barrier = pltpu.get_barrier_semaphore()
    pl.semaphore_signal(barrier, inc=1, device_id={"ctx": partner}, device_id_type=MESH)

    @pl.when(has_up)
    def _():
        pl.semaphore_signal(barrier, inc=1, device_id={"ctx": up}, device_id_type=MESH)

    @pl.when(has_down)
    def _():
        pl.semaphore_signal(barrier, inc=1, device_id={"ctx": down}, device_id_type=MESH)

    pl.semaphore_wait(barrier, 1 + has_up.astype(jnp.int32) + has_down.astype(jnp.int32))

    co[own] = jnp.zeros((rows, GROUP), f32)
    ao[own] = jnp.zeros((rows, GROUP), f32)

    @pl.when(jnp.logical_not(has_down))
    def _():
        hx[...] = jnp.zeros(hx.shape, bf16)

    @pl.when(jnp.logical_not(has_up))
    def _():
        gw[...] = jnp.zeros(gw.shape, bf16)

    def lanes(which, c):
        return pl.ds(pl.multiple_of(which * half + c * GROUP, GROUP), GROUP)

    def x_copy(c):
        return copy_to(
            x_ref.at[:, :, lanes(1 - side, c)], xr.at[c], y_send.at[0, c], y_recv.at[0, c], partner
        )

    def w_copy(c):
        return copy_to(ws.at[c], wr.at[c], y_send.at[1, c], y_recv.at[1, c], partner)

    def c_copy(c):
        return copy_to(sc.at[c], rc.at[c], y_send.at[2, c], y_recv.at[2, c], partner)

    def a_copy(c):
        return copy_to(sa.at[c], ra.at[c], y_send.at[3, c], y_recv.at[3, c], partner)

    def x_up(c, part):
        span = pl.ds(0, LO) if part == 0 else pl.ds(LO, reach - LO)
        return copy_to(
            sx.at[c, span], hx.at[c, span], z_send.at[part, c], z_recv.at[part, c], up
        )

    def w_down(c, part):
        span = pl.ds(0, LO) if part == 0 else pl.ds(LO, reach - LO)
        return copy_to(
            tw.at[c, span], gw.at[c, span], z_send.at[2 + part, c], z_recv.at[2 + part, c], down
        )

    def weigh(j, which, c):
        at = lanes(which, c)
        return (gate_ref[j, :, at].astype(f32) * cot_ref[j, :, at].astype(f32)).astype(bf16)

    def launch(c):
        x_copy(c).start()
        for j in range(slots):
            ws[c, j] = weigh(j, 1 - side, c)
        w_copy(c).start()

    def send_halo(c, part):
        for q in range(LO) if part == 0 else range(LO, reach):
            sx[c, q] = cx[c, tab[t_s + q]]
            tw[c, q] = cw[c, tab[t_t + q]]

        @pl.when(has_up)
        def _():
            x_up(c, part).start()

        @pl.when(has_down)
        def _():
            w_down(c, part).start()

    def take_halo(c, part):
        @pl.when(has_down)
        def _():
            x_up(c, part).wait_recv()

        @pl.when(has_up)
        def _():
            w_down(c, part).wait_recv()

        for q in range(LO) if part == 0 else range(LO, reach):
            cx[c, own + q] = hx[c, q]
            cw[c, own + q] = gw[c, q]

    def gather_pair(c):
        mine, theirs = side * slots, (1 - side) * slots
        for j in range(slots):
            cx[c, mine + j] = x_ref[j, :, lanes(side, c)]
            cw[c, mine + j] = weigh(j, side, c)
        x_copy(c).wait_recv()
        w_copy(c).wait_recv()
        for j in range(slots):
            cx[c, theirs + j] = xr[c, j]
            cw[c, theirs + j] = wr[c, j]
        send_halo(c, 0)

    def relay(c):
        take_halo(c, 0)
        send_halo(c, 1)

    def work(c):
        row = lax.broadcasted_iota(jnp.int32, (rows, GROUP), 0)
        lane = lax.broadcasted_iota(jnp.int32, (rows, GROUP), 1)
        lower, upper = row >= lane, lane >= row
        before_a = jnp.zeros((rows, GROUP), f32)
        before_b = jnp.zeros((rows, GROUP), f32)
        for k in range(lags):
            now_a = pltpu.roll(
                jnp.broadcast_to(rtaps_ref[c, k : k + 1, :], (rows, GROUP)),
                0, 1, stride=1, stride_axis=0,
            )
            now_b = pltpu.roll(
                jnp.broadcast_to(taps_ref[c, k : k + 1, :], (rows, GROUP)),
                0, 1, stride=1, stride_axis=0,
            )
            at = pl.ds((lags - 1 - k) * GROUP, GROUP)
            mat_a[:, at] = jnp.where(lower, now_a, before_a).astype(bf16)
            mat_b[:, pl.ds(k * GROUP, GROUP)] = jnp.where(upper, now_b, before_b).astype(bf16)
            before_a, before_b = now_a, now_b

        take_halo(c, 1)

        def fill(cur, base, mask):
            for r in range(own + reach):
                tile = cur[c, tab[base + r]].reshape(rows // 16, 16, GROUP)
                for u in range(max(0, r - reach), min(own, r + 1)):
                    b = r - u
                    masked = tile * mask[u * lags + b][None]
                    rhs[pl.ds(b * rows, rows), pl.ds(u * GROUP, GROUP)] = masked.reshape(rows, GROUP)

        fill(cw, t_v, bmask_ref)
        out = jnp.dot(mat_b[...], rhs[...], preferred_element_type=f32)
        for u in range(own):
            ao[u] = out[:, u * GROUP : (u + 1) * GROUP]
            vv[:, pl.ds(u * GROUP, GROUP)] = cw[c, tab[t_v + u]]
        for j in range(slots):
            ig_ref[j, :, lanes(side, c)] = ao[tab[t_mine + j]].astype(bf16)
            sa[c, j] = ao[tab[t_theirs + j]].astype(bf16)
        a_copy(c).start()
        fill(cx, t_w, fmask_ref)
        out = jnp.dot(mat_a[...], rhs[...], preferred_element_type=f32)
        for u in range(own):
            co[u] = out[:, u * GROUP : (u + 1) * GROUP]
        for j in range(slots):
            at = lanes(side, c)
            gg_ref[j, :, at] = (cot_ref[j, :, at].astype(f32) * co[tab[t_mine + j]]).astype(bf16)
            sc[c, j] = co[tab[t_theirs + j]].astype(bf16)
        c_copy(c).start()
        flip = (row + lane == rows - 1).astype(f32).astype(bf16)
        turned = jnp.dot(flip, vv[...], preferred_element_type=f32).astype(bf16)
        square = lax.dot_general(
            turned, rhs[...], (((1,), (1,)), ((), ())), preferred_element_type=f32
        )
        for k in range(lags):
            here = square[:, (lags - 1 - k) * rows : (lags - k) * rows]
            if k < lags - 1:
                above = square[:, (lags - 2 - k) * rows : (lags - 1 - k) * rows]
            else:
                above = jnp.zeros_like(here)
            skewed = pltpu.roll(
                jnp.where(row + lane <= rows - 1, here, above), 0, 1, stride=1, stride_axis=0
            )
            fg_ref[c, k : k + 1, :] = jnp.sum(skewed, axis=0, keepdims=True)

    def finish(c):
        a_copy(c).wait_recv()
        c_copy(c).wait_recv()
        at = lanes(1 - side, c)
        for j in range(slots):
            ig_ref[j, :, at] = ra[c, j]
            gg_ref[j, :, at] = (
                cot_ref[j, :, at].astype(f32) * rc[c, j].astype(f32)
            ).astype(bf16)

    for c in range(min(LEAD, chunks)):
        launch(c)

    @pl.loop(0, chunks + 3)
    def _(s):
        if LEAD < chunks:
            @pl.when(s + LEAD < chunks)
            def _():
                launch(s + LEAD)

        @pl.when(s < chunks)
        def _():
            gather_pair(s)

        @pl.when((s >= 1) & (s < chunks + 1))
        def _():
            relay(s - 1)

        @pl.when((s >= 2) & (s < chunks + 2))
        def _():
            work(s - 2)

        @pl.when(s >= 3)
        def _():
            finish(s - 3)

    @pl.loop(0, chunks)
    def _(c):
        x_copy(c).wait_send()
        w_copy(c).wait_send()
        a_copy(c).wait_send()
        c_copy(c).wait_send()

        @pl.when(has_up)
        def _():
            x_up(c, 0).wait_send()
            x_up(c, 1).wait_send()

        @pl.when(has_down)
        def _():
            w_down(c, 0).wait_send()
            w_down(c, 1).wait_send()


def tables(tile_owner, support, n_ctx, slots, me):
    total = tile_owner.shape[0]
    maxlag = support.shape[1]
    own, reach = 2 * slots, maxlag - 1
    pair, side = me // 2, me % 2
    count0 = jnp.sum((tile_owner == 2 * pair).astype(jnp.int32))
    count1 = jnp.sum((tile_owner == 2 * pair + 1).astype(jnp.int32))
    first = jnp.sum((tile_owner < 2 * pair).astype(jnp.int32))
    n = count0 + count1

    def place(u):
        return jnp.clip(jnp.where(u < count0, u, slots + u - count0), 0, own - 1)

    q = jnp.arange(reach, dtype=jnp.int32)
    r = jnp.arange(own + reach, dtype=jnp.int32)
    j = jnp.arange(slots, dtype=jnp.int32)
    last = own + reach - 1
    t_s = jnp.where(q < n, place(n - 1 - q), jnp.clip(own + q - n, 0, last))
    t_t = jnp.where(q < n, place(q), jnp.clip(own + q - n, 0, last))
    t_w = jnp.where(r < reach, own + reach - 1 - r, place(r - reach))
    t_v = jnp.where(r < n, place(r), jnp.clip(own + r - n, 0, last))
    u0 = jnp.where(j < count0, j, own)
    u1 = jnp.where(j < count1, j + count0, own)
    t_mine = jnp.where(side == 0, u0, u1)
    t_theirs = jnp.where(side == 0, u1, u0)
    tab = jnp.concatenate([t_s, t_t, t_w, t_v, t_mine, t_theirs]).astype(jnp.int32)

    u = jnp.arange(own, dtype=jnp.int32)[:, None]
    k = jnp.arange(maxlag, dtype=jnp.int32)[None, :]
    live = u < n
    reader = first + u
    ok_f = live & (support[jnp.clip(reader, 0, total - 1), k] >= 0)
    later = reader + k
    ok_b = live & (later < total) & (support[jnp.clip(later, 0, total - 1), k] >= 0)
    spread = lambda ok: jnp.broadcast_to(
        ok.reshape(-1)[:, None, None], (own * maxlag, 16, GROUP)
    ).astype(jnp.bfloat16)
    return tab, spread(ok_f[:, ::-1]), spread(ok_b)


def per_device(conv_input, gate_signal, cotangent, filters, tile_owner, support):
    slots, rows, channels = conv_input.shape
    lags = support.shape[1]
    filter_count, taps = filters.shape
    n_ctx = lax.axis_size("ctx")
    me = lax.axis_index("ctx")
    half = channels // 2
    chunks = half // GROUP
    own, reach = 2 * slots, lags - 1
    tab, fmask, bmask = tables(tile_owner, support, n_ctx, slots, me)
    turn = lambda a: jnp.roll(a[..., ::-1], 1, axis=-1)
    narrow = filters.astype(jnp.bfloat16).astype(jnp.float32)
    at = (me % 2) * chunks
    mine = lax.dynamic_slice_in_dim(narrow, at, chunks, 0).reshape(chunks, lags, rows)
    bf16, f32 = jnp.bfloat16, jnp.float32
    vmem = pl.BlockSpec(memory_space=pltpu.VMEM)
    whole = jax.ShapeDtypeStruct(conv_input.shape, bf16)
    part = lambda count: pltpu.VMEM((chunks, count, rows, GROUP), bf16)
    gate_grad, input_grad, sums = pl.pallas_call(
        functools.partial(kernel, n_ctx),
        out_shape=(whole, whole, jax.ShapeDtypeStruct((chunks, lags, rows), f32)),
        in_specs=[pl.BlockSpec(memory_space=pltpu.SMEM)] + [vmem] * 7,
        out_specs=(vmem, vmem, vmem),
        scratch_shapes=[
            part(slots),
            part(slots),
            part(slots),
            part(reach),
            part(reach),
            part(reach),
            part(reach),
            part(slots),
            part(slots),
            part(slots),
            part(slots),
            part(own + reach),
            part(own + reach),
            pltpu.VMEM((rows, lags * rows), bf16),
            pltpu.VMEM((rows, lags * rows), bf16),
            pltpu.VMEM((lags * rows, own * GROUP), bf16),
            pltpu.VMEM((rows, own * GROUP), bf16),
            pltpu.VMEM((own + 1, rows, GROUP), f32),
            pltpu.VMEM((own + 1, rows, GROUP), f32),
            pltpu.SemaphoreType.DMA((4, chunks)),
            pltpu.SemaphoreType.DMA((4, chunks)),
            pltpu.SemaphoreType.DMA((4, chunks)),
            pltpu.SemaphoreType.DMA((4, chunks)),
        ],
        compiler_params=pltpu.CompilerParams(
            collective_id=0, has_side_effects=True, vmem_limit_bytes=56 * 2**20
        ),
        cost_estimate=pl.CostEstimate(
            flops=6 * rows * rows * own * lags * half,
            bytes_accessed=10 * slots * rows * channels,
            transcendentals=0,
        ),
    )(tab, conv_input, gate_signal, cotangent, mine, turn(mine), fmask, bmask)
    norm = 1.0 / math.sqrt(
        tile_owner.shape[0] * rows * channels * lax.axis_size("ch") / filter_count
    )
    local = jnp.zeros((filter_count, taps), f32)
    local = lax.dynamic_update_slice_in_dim(
        local, sums[..., ::-1].reshape(chunks, taps), at, 0
    )
    filter_grad = lax.psum(local, ("ctx", "ch")) * norm
    return gate_grad, input_grad, filter_grad


def solution(mesh):
    return jax.shard_map(
        per_device,
        mesh=mesh,
        in_specs=(P("ctx", None, "ch"), P("ctx", None, "ch"), P("ctx", None, "ch"), P(), P(), P()),
        out_specs=(P("ctx", None, "ch"), P("ctx", None, "ch"), P()),
        check_vma=False,
    )
```

time: 1290 us -> 255 us (0.20)
  the two profiles are of different devices: /device:TPU:12 before, /device:TPU:0 now
where the time goes in v1:
time: 255 us; the launch traced here: 254 us
  waiting for transfers between devices  118 us (46%)
  Pallas kernels  101 us (40%)
  between operations  15.4 us (6%)
  local copies, waits for them, and re-layouts  10.6 us (4%)
  other arithmetic  8.44 us (3%)
    psum x1, waiting for transfers between devices, per_device(): filter_grad = lax.psum(local, ('ctx', 'ch')) * norm  118 us
    pallas_call x1, Pallas kernels, per_device(): pl.pallas_call(functools.partial(kernel, n_ctx), out_shape=(whole, whole,...  101 us
    unnamed x11, local copies, waits for them, and re-layouts  5.28 us
  transfers between devices with their start and end apart: 1, of which 1 were waited for; matrix products, arithmetic and copies ran while one was open for 0% of the time, Pallas kernels for 0%

profile of v1, /device:TPU:0, one launch (start us, length us, event | category | flops | bytes accessed | tf_op | source)
XLA Modules:
  0.0 253.8 jit_solution(13454307763309066575)
XLA Ops:
  7.2 0.0 copy-start
  7.2 0.0 all-reduce.2.cloned.1.call-start
  7.2 1.3 fusion.11
  8.6 0.7 fusion.15
  9.2 0.7 iota_add_fusion
  11.2 0.7 compare_select_fusion.7
  11.9 0.1 fusion.3
  11.9 0.1 reshape.120
  12.0 0.1 fusion.2
  12.1 0.1 reshape.126
  12.2 0.0 copy-done
  12.2 0.7 gather_fusion
  12.9 0.7 gather_fusion.1
  13.7 0.1 reshape.133
  13.7 0.1 reshape.135
  13.8 0.1 fusion.6
  13.9 0.1 rev.7
  14.0 0.1 reshape.118
  14.1 0.1 reshape.119
  14.2 0.8 convert_bitcast_fusion
  15.0 0.0 copy-start.2
  15.0 0.1 slice.20
  15.1 0.1 slice.14
  15.1 1.3 broadcast_select_fusion
  16.5 0.7 compare_select_fusion.10
  17.1 0.7 pad_maximum_fusion.rtaps_ref
  17.8 0.6 concatenate.13.tab
  18.4 0.8 broadcast_in_dim.20.fmask_ref
  19.2 0.8 broadcast_in_dim.41.bmask_ref
  20.1 0.0 copy-done.2
  20.1 101.4 %shard_map.85 = (bf16[4,128,2048]{2,1,0:T(8,128)(2,1)}, bf16[4,128,2048]{2,1,0:T(8,128)(2,1)}, f32[8,8,128]{2,1,0:T(8,128)}) custom-call(s32[52]{0:T(128)} %concatenate.13.tab, bf16[4,128,2048]{2,1,0:T(8,128)(2,1)} %x_ref.1, bf16[4,128,2048]{2,1,0:T(8,128)(2,1)} %gate_ref.1, bf16[4,128,2048]{2,1,0:T(8,128)(2,1)} %cot_ref.1, f32[8,8,128]{2,1,0:T(8,128)} %bitcast.15, ...), custom_call_target="tpu_custom_call" | custom-call | flops 6442450944 | bytes 10485760 | tf_op jit(solution)/shard_map/pallas_call | solution.py:362
  121.5 0.8 rev.8
  122.4 0.0 copy-start.3
  122.4 0.6 copy-done.3
  123.0 0.0 all-reduce.2.cloned.1.call-update
  123.0 117.9 %all-reduce.2.cloned.1.call-done = f32[16,1024]{1,0:T(8,128)} async-done(((f32[16,1024]{1,0:T(8,128)}), f32[16,1024]{1,0:T(8,128)}) %all-reduce.2.cloned.1.call-update) | async-done | bytes 65552 | tf_op jit(solution)/shard_map/psum | solution.py:408
  240.9 1.5 broadcast_multiply_fusion
  242.4 0.0 copy-start.1
  242.4 3.3 %copy.18 = bf16[4,128,2048]{2,1,0:T(8,128)(2,1)} copy(bf16[4,128,2048]{2,1,0:T(8,128)(2,1)} %get-tuple-element.25) | data formatting | bytes 4194304
  245.7 0.0 copy-done.1
  245.7 1.3 copy.19
  (6 shorter events, 0.1 us)
Async XLA Ops:
  7.2 5.0 %copy-start = (s32[24,8]{0,1:T(8,128)S(1)}, s32[24,8]{0,1:T(8,128)}, u32[]{:S(2)}) copy-start(s32[24,8]{0,1:T(8,128)} %param.11) | copy-start | bytes 2308
  7.2 233.7 %all-reduce.2.cloned.1.call-start = ((), (), s32[]{:S(2)}) async-start(), calls=%async_computation | async-start | bytes 131072 | tf_op jit(solution)/shard_map/psum | solution.py:408
  15.0 5.1 %copy-start.2 = (f32[1,8,8,128]{3,2,1,0:T(8,128)}, f32[1,8,8,128]{3,2,1,0:T(8,128)S(1)}, u32[]{:S(2)}) copy-start(f32[1,8,8,128]{3,2,1,0:T(8,128)S(1)} %copy.13) | copy-start | bytes 98308
  122.4 0.6 copy-start.3
  242.4 3.3 %copy-start.1 = (bf16[4,128,2048]{2,1,0:T(8,128)(2,1)S(1)}, bf16[4,128,2048]{2,1,0:T(8,128)(2,1)}, u32[]{:S(2)}) copy-start(bf16[4,128,2048]{2,1,0:T(8,128)(2,1)} %get-tuple-element.26) | copy-start | bytes 6291460
Sparse Core Ops, SparseCore 0:
  123.1 117.7 all-reduce.1

commit v2 on v1

--- a/solution.py
+++ b/solution.py
@@ -9,32 +9,34 @@
 from jax.sharding import PartitionSpec as P
 
 GROUP = 128
-LEAD = 8
+LEAD = 4
+LAG = 5
+LATE = 2
 LO = 4
 MESH = pl.DeviceIdType.MESH
 
 
-def copy_to(src, dst, send, recv, ctx):
+def copy_to(src, dst, send, recv, to, axis="ctx"):
     return pltpu.make_async_remote_copy(
         src_ref=src,
         dst_ref=dst,
         send_sem=send,
         recv_sem=recv,
-        device_id={"ctx": ctx},
+        device_id={axis: to},
         device_id_type=MESH,
     )
 
 
 def kernel(
     n_ctx,
-    tab,
+    n_ch,
+    norm,
+    owner_ref,
+    support_ref,
     x_ref,
     gate_ref,
     cot_ref,
     taps_ref,
-    rtaps_ref,
-    fmask_ref,
-    bmask_ref,
     gg_ref,
     ig_ref,
     fg_ref,
@@ -57,15 +59,28 @@
     vv,
     co,
     ao,
+    tab,
+    taps,
+    fmask_ref,
+    bmask_ref,
+    sums,
+    ch_sums,
+    ch_got,
+    ctx_got,
     y_send,
     y_recv,
     z_send,
     z_recv,
+    ch_send,
+    ch_recv,
+    ctx_send,
+    ctx_recv,
 ):
     slots, rows, channels = x_ref.shape
     half = channels // 2
     chunks = half // GROUP
-    lags = taps_ref.shape[1]
+    lags = support_ref.shape[1]
+    total = owner_ref.shape[0]
     own = 2 * slots
     reach = lags - 1
     f32, bf16 = jnp.float32, jnp.bfloat16
@@ -78,18 +93,27 @@
     has_down = pair > 0
     t_s, t_t, t_w, t_v, t_mine, t_theirs = 0, 7, 14, 29, 44, 48
 
+    my_ch = lax.axis_index("ch")
+    batches = [(0, chunks - LATE), (chunks - LATE, LATE)]
+
+    def other(d, axis, mine, size):
+        return {axis: lax.rem(mine + d, size)}
+
     barrier = pltpu.get_barrier_semaphore()
-    pl.semaphore_signal(barrier, inc=1, device_id={"ctx": partner}, device_id_type=MESH)
-
-    @pl.when(has_up)
-    def _():
-        pl.semaphore_signal(barrier, inc=1, device_id={"ctx": up}, device_id_type=MESH)
-
-    @pl.when(has_down)
-    def _():
-        pl.semaphore_signal(barrier, inc=1, device_id={"ctx": down}, device_id_type=MESH)
-
-    pl.semaphore_wait(barrier, 1 + has_up.astype(jnp.int32) + has_down.astype(jnp.int32))
+
+    @pl.loop(1, n_ctx)
+    def _(d):
+        pl.semaphore_signal(
+            barrier, inc=1, device_id=other(d, "ctx", me, n_ctx), device_id_type=MESH
+        )
+
+    @pl.loop(1, n_ch)
+    def _(d):
+        pl.semaphore_signal(
+            barrier, inc=1, device_id=other(d, "ch", my_ch, n_ch), device_id_type=MESH
+        )
+
+    pl.semaphore_wait(barrier, n_ctx + n_ch - 2)
 
     co[own] = jnp.zeros((rows, GROUP), f32)
     ao[own] = jnp.zeros((rows, GROUP), f32)
@@ -186,22 +210,18 @@
     def work(c):
         row = lax.broadcasted_iota(jnp.int32, (rows, GROUP), 0)
         lane = lax.broadcasted_iota(jnp.int32, (rows, GROUP), 1)
-        lower, upper = row >= lane, lane >= row
-        before_a = jnp.zeros((rows, GROUP), f32)
-        before_b = jnp.zeros((rows, GROUP), f32)
+        upper = lane >= row
+        before = jnp.zeros((rows, GROUP), f32)
         for k in range(lags):
-            now_a = pltpu.roll(
-                jnp.broadcast_to(rtaps_ref[c, k : k + 1, :], (rows, GROUP)),
+            now = pltpu.roll(
+                jnp.broadcast_to(taps[c, k : k + 1, :], (rows, GROUP)),
                 0, 1, stride=1, stride_axis=0,
             )
-            now_b = pltpu.roll(
-                jnp.broadcast_to(taps_ref[c, k : k + 1, :], (rows, GROUP)),
-                0, 1, stride=1, stride_axis=0,
-            )
+            block = jnp.where(upper, now, before)
             at = pl.ds((lags - 1 - k) * GROUP, GROUP)
-            mat_a[:, at] = jnp.where(lower, now_a, before_a).astype(bf16)
-            mat_b[:, pl.ds(k * GROUP, GROUP)] = jnp.where(upper, now_b, before_b).astype(bf16)
-            before_a, before_b = now_a, now_b
+            mat_a[:, at] = block.T.astype(bf16)
+            mat_b[:, pl.ds(k * GROUP, GROUP)] = block.astype(bf16)
+            before = now
 
         take_halo(c, 1)
 
@@ -245,7 +265,7 @@
             skewed = pltpu.roll(
                 jnp.where(row + lane <= rows - 1, here, above), 0, 1, stride=1, stride_axis=0
             )
-            fg_ref[c, k : k + 1, :] = jnp.sum(skewed, axis=0, keepdims=True)
+            sums[c, k : k + 1, :] = jnp.sum(skewed, axis=0, keepdims=True)
 
     def finish(c):
         a_copy(c).wait_recv()
@@ -257,10 +277,138 @@
                 cot_ref[j, :, at].astype(f32) * rc[c, j].astype(f32)
             ).astype(bf16)
 
+    def over_ch(b, d, sender):
+        start, size = batches[b]
+        return copy_to(
+            sums.at[pl.ds(start, size)],
+            ch_got.at[sender, pl.ds(start, size)],
+            ch_send.at[b, d],
+            ch_recv.at[b, sender],
+            lax.rem(my_ch + d, n_ch),
+            "ch",
+        )
+
+    def over_ctx(b, d, sender):
+        start, size = batches[b]
+        return copy_to(
+            ch_sums.at[pl.ds(start, size)],
+            ctx_got.at[sender, pl.ds(start, size)],
+            ctx_send.at[b, d],
+            ctx_recv.at[b, sender],
+            lax.rem(me + d, n_ctx),
+        )
+
+    def sum_over_ch(b):
+        @pl.loop(1, n_ch)
+        def _(d):
+            over_ch(b, d, my_ch).start()
+
+        at = pl.ds(*batches[b])
+        ch_got[my_ch, at] = sums[at]
+
+    def sum_over_ctx(b):
+        @pl.loop(1, n_ch)
+        def _(d):
+            over_ch(b, d, lax.rem(my_ch + d, n_ch)).wait_recv()
+
+        at = pl.ds(*batches[b])
+        acc = ch_got[0, at]
+        for i in range(1, n_ch):
+            acc = acc + ch_got[i, at]
+        ch_sums[at] = acc
+
+        @pl.loop(1, n_ctx)
+        def _(d):
+            over_ctx(b, d, me).start()
+
+        ctx_got[me, at] = acc
+
+    def end_sums():
+        for b in range(2):
+            @pl.loop(1, n_ctx)
+            def _(d):
+                over_ctx(b, d, lax.rem(me + d, n_ctx)).wait_recv()
+
+        row = lax.broadcasted_iota(jnp.int32, (GROUP, GROUP), 0)
+        lane = lax.broadcasted_iota(jnp.int32, (GROUP, GROUP), 1)
+        flip = (row + lane == GROUP - 1).astype(f32)
+        for parity in range(2):
+            acc = lax.fori_loop(
+                1,
+                n_ctx // 2,
+                lambda i, acc: acc + ctx_got[2 * i + parity],
+                ctx_got[parity],
+            )
+            flat = jnp.dot(
+                acc.reshape(chunks * lags, GROUP),
+                flip,
+                preferred_element_type=f32,
+                precision=lax.Precision.HIGHEST,
+            )
+            whole = flat.reshape(chunks, lags, GROUP) * norm
+            for c in range(chunks):
+                for k in range(lags):
+                    fg_ref[
+                        parity * chunks + c : parity * chunks + c + 1,
+                        k * GROUP : (k + 1) * GROUP,
+                    ] = whole[c, k : k + 1]
+
+    def make_tables():
+        def count(t, found):
+            holder = owner_ref[t]
+            one = lambda hit: hit.astype(jnp.int32)
+            return (
+                found[0] + one(holder == 2 * pair),
+                found[1] + one(holder == 2 * pair + 1),
+                found[2] + one(holder < 2 * pair),
+            )
+
+        zero = jnp.int32(0)
+        count0, count1, first = lax.fori_loop(0, total, count, (zero, zero, zero))
+        n = count0 + count1
+
+        mine = taps_ref[pl.ds(pl.multiple_of(side * chunks, chunks), chunks), :]
+        mine = mine.astype(bf16).astype(f32)
+        for c in range(chunks):
+            for k in range(lags):
+                taps[c, k : k + 1, :] = mine[c : c + 1, k * GROUP : (k + 1) * GROUP]
+
+        def place(u):
+            return jnp.clip(jnp.where(u < count0, u, slots + u - count0), 0, own - 1)
+
+        def beyond(q):
+            return jnp.clip(own + q - n, 0, own + reach - 1)
+
+        for q in range(reach):
+            tab[t_s + q] = jnp.where(q < n, place(n - 1 - q), beyond(q))
+            tab[t_t + q] = jnp.where(q < n, place(q), beyond(q))
+        for r in range(own + reach):
+            tab[t_w + r] = own + reach - 1 - r if r < reach else place(r - reach)
+            tab[t_v + r] = jnp.where(r < n, place(r), beyond(r))
+        for j in range(slots):
+            at0 = jnp.where(j < count0, j, own)
+            at1 = jnp.where(j < count1, j + count0, own)
+            tab[t_mine + j] = jnp.where(side == 0, at0, at1)
+            tab[t_theirs + j] = jnp.where(side == 0, at1, at0)
+
+        def put(mask, at, ok):
+            value = ok.astype(jnp.int32).astype(f32)
+            mask[at] = jnp.full((16, GROUP), value, f32).astype(bf16)
+
+        for u in range(own):
+            for k in range(lags):
+                live = u < n
+                found = support_ref[jnp.clip(first + u, 0, total - 1), k] >= 0
+                put(fmask_ref, u * lags + lags - 1 - k, live & found)
+                later = first + u + k
+                found = support_ref[jnp.clip(later, 0, total - 1), k] >= 0
+                put(bmask_ref, u * lags + k, live & found & (later < total))
+
     for c in range(min(LEAD, chunks)):
         launch(c)
-
-    @pl.loop(0, chunks + 3)
+    make_tables()
+
+    @pl.loop(0, chunks + LAG)
     def _(s):
         if LEAD < chunks:
             @pl.when(s + LEAD < chunks)
@@ -279,9 +427,28 @@
         def _():
             work(s - 2)
 
-        @pl.when(s >= 3)
-        def _():
-            finish(s - 3)
+        for b, (start, size) in enumerate(batches):
+            @pl.when(s == start + size + 1)
+            def _():
+                sum_over_ch(b)
+
+            @pl.when(s == start + size + 2)
+            def _():
+                sum_over_ctx(b)
+
+        @pl.when(s >= LAG)
+        def _():
+            finish(s - LAG)
+
+    end_sums()
+    for b in range(2):
+        @pl.loop(1, n_ch)
+        def _(d):
+            over_ch(b, d, my_ch).wait_send()
+
+        @pl.loop(1, n_ctx)
+        def _(d):
+            over_ctx(b, d, me).wait_send()
 
     @pl.loop(0, chunks)
     def _(c):
@@ -301,68 +468,26 @@
             w_down(c, 1).wait_send()
 
 
-def tables(tile_owner, support, n_ctx, slots, me):
-    total = tile_owner.shape[0]
-    maxlag = support.shape[1]
-    own, reach = 2 * slots, maxlag - 1
-    pair, side = me // 2, me % 2
-    count0 = jnp.sum((tile_owner == 2 * pair).astype(jnp.int32))
-    count1 = jnp.sum((tile_owner == 2 * pair + 1).astype(jnp.int32))
-    first = jnp.sum((tile_owner < 2 * pair).astype(jnp.int32))
-    n = count0 + count1
-
-    def place(u):
-        return jnp.clip(jnp.where(u < count0, u, slots + u - count0), 0, own - 1)
-
-    q = jnp.arange(reach, dtype=jnp.int32)
-    r = jnp.arange(own + reach, dtype=jnp.int32)
-    j = jnp.arange(slots, dtype=jnp.int32)
-    last = own + reach - 1
-    t_s = jnp.where(q < n, place(n - 1 - q), jnp.clip(own + q - n, 0, last))
-    t_t = jnp.where(q < n, place(q), jnp.clip(own + q - n, 0, last))
-    t_w = jnp.where(r < reach, own + reach - 1 - r, place(r - reach))
-    t_v = jnp.where(r < n, place(r), jnp.clip(own + r - n, 0, last))
-    u0 = jnp.where(j < count0, j, own)
-    u1 = jnp.where(j < count1, j + count0, own)
-    t_mine = jnp.where(side == 0, u0, u1)
-    t_theirs = jnp.where(side == 0, u1, u0)
-    tab = jnp.concatenate([t_s, t_t, t_w, t_v, t_mine, t_theirs]).astype(jnp.int32)
-
-    u = jnp.arange(own, dtype=jnp.int32)[:, None]
-    k = jnp.arange(maxlag, dtype=jnp.int32)[None, :]
-    live = u < n
-    reader = first + u
-    ok_f = live & (support[jnp.clip(reader, 0, total - 1), k] >= 0)
-    later = reader + k
-    ok_b = live & (later < total) & (support[jnp.clip(later, 0, total - 1), k] >= 0)
-    spread = lambda ok: jnp.broadcast_to(
-        ok.reshape(-1)[:, None, None], (own * maxlag, 16, GROUP)
-    ).astype(jnp.bfloat16)
-    return tab, spread(ok_f[:, ::-1]), spread(ok_b)
-
-
 def per_device(conv_input, gate_signal, cotangent, filters, tile_owner, support):
     slots, rows, channels = conv_input.shape
     lags = support.shape[1]
     filter_count, taps = filters.shape
     n_ctx = lax.axis_size("ctx")
-    me = lax.axis_index("ctx")
+    n_ch = lax.axis_size("ch")
     half = channels // 2
     chunks = half // GROUP
     own, reach = 2 * slots, lags - 1
-    tab, fmask, bmask = tables(tile_owner, support, n_ctx, slots, me)
-    turn = lambda a: jnp.roll(a[..., ::-1], 1, axis=-1)
-    narrow = filters.astype(jnp.bfloat16).astype(jnp.float32)
-    at = (me % 2) * chunks
-    mine = lax.dynamic_slice_in_dim(narrow, at, chunks, 0).reshape(chunks, lags, rows)
+    norm = 1.0 / math.sqrt(
+        tile_owner.shape[0] * rows * channels * lax.axis_size("ch") / filter_count
+    )
     bf16, f32 = jnp.bfloat16, jnp.float32
     vmem = pl.BlockSpec(memory_space=pltpu.VMEM)
     whole = jax.ShapeDtypeStruct(conv_input.shape, bf16)
     part = lambda count: pltpu.VMEM((chunks, count, rows, GROUP), bf16)
-    gate_grad, input_grad, sums = pl.pallas_call(
-        functools.partial(kernel, n_ctx),
-        out_shape=(whole, whole, jax.ShapeDtypeStruct((chunks, lags, rows), f32)),
-        in_specs=[pl.BlockSpec(memory_space=pltpu.SMEM)] + [vmem] * 7,
+    return pl.pallas_call(
+        functools.partial(kernel, n_ctx, n_ch, norm),
+        out_shape=(whole, whole, jax.ShapeDtypeStruct(filters.shape, f32)),
+        in_specs=[pl.BlockSpec(memory_space=pltpu.SMEM)] * 2 + [vmem] * 4,
         out_specs=(vmem, vmem, vmem),
         scratch_shapes=[
             part(slots),
@@ -384,10 +509,22 @@
             pltpu.VMEM((rows, own * GROUP), bf16),
             pltpu.VMEM((own + 1, rows, GROUP), f32),
             pltpu.VMEM((own + 1, rows, GROUP), f32),
+            pltpu.SMEM((52,), jnp.int32),
+            pltpu.VMEM((chunks, lags, GROUP), f32),
+            pltpu.VMEM((own * lags, 16, GROUP), bf16),
+            pltpu.VMEM((own * lags, 16, GROUP), bf16),
+            pltpu.VMEM((chunks, lags, GROUP), f32),
+            pltpu.VMEM((chunks, lags, GROUP), f32),
+            pltpu.VMEM((n_ch, chunks, lags, GROUP), f32),
+            pltpu.VMEM((n_ctx, chunks, lags, GROUP), f32),
             pltpu.SemaphoreType.DMA((4, chunks)),
             pltpu.SemaphoreType.DMA((4, chunks)),
             pltpu.SemaphoreType.DMA((4, chunks)),
             pltpu.SemaphoreType.DMA((4, chunks)),
+            pltpu.SemaphoreType.DMA((2, n_ch)),
+            pltpu.SemaphoreType.DMA((2, n_ch)),
+            pltpu.SemaphoreType.DMA((2, n_ctx)),
+            pltpu.SemaphoreType.DMA((2, n_ctx)),
         ],
         compiler_params=pltpu.CompilerParams(
             collective_id=0, has_side_effects=True, vmem_limit_bytes=56 * 2**20
@@ -397,16 +534,7 @@
             bytes_accessed=10 * slots * rows * channels,
             transcendentals=0,
         ),
-    )(tab, conv_input, gate_signal, cotangent, mine, turn(mine), fmask, bmask)
-    norm = 1.0 / math.sqrt(
-        tile_owner.shape[0] * rows * channels * lax.axis_size("ch") / filter_count
-    )
-    local = jnp.zeros((filter_count, taps), f32)
-    local = lax.dynamic_update_slice_in_dim(
-        local, sums[..., ::-1].reshape(chunks, taps), at, 0
-    )
-    filter_grad = lax.psum(local, ("ctx", "ch")) * norm
-    return gate_grad, input_grad, filter_grad
+    )(tile_owner, support, conv_input, gate_signal, cotangent, filters)
 
 
 def solution(mesh):

time: 255 us -> 115 us (0.45)
  waiting for transfers between devices: 118 us -> 0 us
  between operations: 15.4 us -> 0.65 us
  other arithmetic: 8.44 us -> 0 us
  Pallas kernels: 101 us -> 107 us
  local copies, waits for them, and re-layouts: 10.6 us -> 6.62 us
    psum x1 -> x0, waiting for transfers between devices: 118 us -> none  [per_device(): filter_grad = lax.psum(local, ('ctx', 'ch')) * norm]
    pallas_call x1, Pallas kernels: 101 us -> 107 us  [per_device(): pl.pallas_call(functools.partial(kernel, n_ctx, n_ch, norm), out_shape=(w...]
    select_n x3 -> x0, other arithmetic: 2.61 us -> none  [the longest x1 1.3 us: tables(): t_theirs = jnp.where(side == 0, u1, u0)]
    unnamed x11 -> x8, local copies, waits for them, and re-layouts: 5.28 us -> 6.62 us
  transfers between devices with their start and end apart: 1 -> 0, of which waited for: 1 -> 0; matrix products, arithmetic and copies ran while one was open for 0% -> 0% of each run, Pallas kernels for 0% -> 0%
where the time goes in v2:
time: 115 us
  Pallas kernels  107 us (93%)
  local copies, waits for them, and re-layouts  6.62 us (6%)
    pallas_call x1, Pallas kernels, per_device(): pl.pallas_call(functools.partial(kernel, n_ctx, n_ch, norm), out_shape=(w...  107 us
    unnamed x8, local copies, waits for them, and re-layouts  6.62 us

profile of v2, /device:TPU:0, one launch (start us, length us, event | category | flops | bytes accessed | tf_op | source)
XLA Modules:
  0.0 114.6 jit_solution(2398635900959909802)
XLA Ops:
  0.6 1.4 %copy.9.support_ref = s32[24,8]{1,0:T(8,128)} copy(s32[24,8]{0,1:T(8,128)} %param.11) | data formatting | bytes 1536 | tf_op args[5]
  2.0 107.4 %shard_map.85 = (bf16[4,128,2048]{2,1,0:T(8,128)(2,1)}, bf16[4,128,2048]{2,1,0:T(8,128)(2,1)}, f32[16,1024]{1,0:T(8,128)}) custom-call(s32[24]{0:T(128)} %owner_ref.1, s32[24,8]{1,0:T(8,128)} %copy.9.support_ref, bf16[4,128,2048]{2,1,0:T(8,128)(2,1)} %x_ref.1, bf16[4,128,2048]{2,1,0:T(8,128)(2,1)} %gate_ref.1, bf16[4,128,2048]{2,1,0:T(8,128)(2,1)} %cot_ref.1, ...), custom_call_target="tpu_custom_call" | custom-call | flops 6442450944 | bytes 10485760 | tf_op jit(solution)/shard_map/pallas_call | solution.py:487
  109.3 0.0 copy-start
  109.4 3.3 %copy.13 = bf16[4,128,2048]{2,1,0:T(8,128)(2,1)} copy(bf16[4,128,2048]{2,1,0:T(8,128)(2,1)} %get-tuple-element.6) | data formatting | bytes 4194304
  112.7 0.0 copy-done
  112.7 0.0 copy-start.1
  112.7 1.3 %copy.14 = bf16[4,128,2048]{2,1,0:T(8,128)(2,1)} copy(bf16[4,128,2048]{2,1,0:T(8,128)(2,1)S(1)} %copy-done) | data formatting | bytes 4194304
  114.0 0.0 copy-done.1
  114.0 0.6 copy.15
Async XLA Ops:
  109.3 3.3 %copy-start = (bf16[4,128,2048]{2,1,0:T(8,128)(2,1)S(1)}, bf16[4,128,2048]{2,1,0:T(8,128)(2,1)}, u32[]{:S(2)}) copy-start(bf16[4,128,2048]{2,1,0:T(8,128)(2,1)} %get-tuple-element.7) | copy-start | bytes 6291460
  112.7 1.3 %copy-start.1 = (f32[16,1024]{1,0:T(8,128)S(1)}, f32[16,1024]{1,0:T(8,128)}, u32[]{:S(2)}) copy-start(f32[16,1024]{1,0:T(8,128)} %get-tuple-element.8) | copy-start | bytes 196612

commit v3 on v2

--- a/solution.py
+++ b/solution.py
@@ -9,7 +9,7 @@
 from jax.sharding import PartitionSpec as P
 
 GROUP = 128
-LEAD = 4
+LEAD = 2
 LAG = 5
 LATE = 2
 LO = 4
@@ -37,9 +37,16 @@
     gate_ref,
     cot_ref,
     taps_ref,
-    gg_ref,
+    conv_ref,
     ig_ref,
     fg_ref,
+    xo,
+    gate_own,
+    gate_far,
+    cot_own,
+    cot_far,
+    conv_own,
+    ig_own,
     xr,
     wr,
     ws,
@@ -75,11 +82,14 @@
     ch_recv,
     ctx_send,
     ctx_recv,
+    in_sem,
+    x_sem,
+    out_sem,
 ):
     slots, rows, channels = x_ref.shape
     half = channels // 2
     chunks = half // GROUP
-    lags = support_ref.shape[1]
+    lags = support_ref.shape[0]
     total = owner_ref.shape[0]
     own = 2 * slots
     reach = lags - 1
@@ -99,6 +109,39 @@
     def other(d, axis, mine, size):
         return {axis: lax.rem(mine + d, size)}
 
+    def lanes(which, c):
+        return pl.ds(pl.multiple_of(which * half + c * GROUP, GROUP), GROUP)
+
+    def load(kind, which, c):
+        src = (gate_ref, cot_ref)[kind]
+        at = 0 if which is side else 1
+        dst = ((gate_own, gate_far), (cot_own, cot_far))[kind][at]
+        return pltpu.make_async_copy(
+            src.at[:, :, lanes(which, c)], dst.at[c], in_sem.at[kind, at, c]
+        )
+
+    def load_x(c):
+        return pltpu.make_async_copy(x_ref.at[:, :, lanes(side, c)], xo.at[c], x_sem.at[c])
+
+    def store(kind, which, c):
+        dst = (conv_ref, ig_ref)[kind].at[:, :, lanes(which, c)]
+        if which is side:
+            src = (conv_own, ig_own)[kind].at[c]
+        else:
+            src = (rc, ra)[kind].at[c]
+        at = 0 if which is side else 1
+        return pltpu.make_async_copy(src, dst, out_sem.at[kind, at, c])
+
+    far = 1 - side
+
+    @pl.loop(0, chunks)
+    def _(c):
+        load(0, far, c).start()
+        load(1, far, c).start()
+        load_x(c).start()
+        load(0, side, c).start()
+        load(1, side, c).start()
+
     barrier = pltpu.get_barrier_semaphore()
 
     @pl.loop(1, n_ctx)
@@ -126,12 +169,9 @@
     def _():
         gw[...] = jnp.zeros(gw.shape, bf16)
 
-    def lanes(which, c):
-        return pl.ds(pl.multiple_of(which * half + c * GROUP, GROUP), GROUP)
-
     def x_copy(c):
         return copy_to(
-            x_ref.at[:, :, lanes(1 - side, c)], xr.at[c], y_send.at[0, c], y_recv.at[0, c], partner
+            x_ref.at[:, :, lanes(far, c)], xr.at[c], y_send.at[0, c], y_recv.at[0, c], partner
         )
 
     def w_copy(c):
@@ -156,13 +196,15 @@
         )
 
     def weigh(j, which, c):
-        at = lanes(which, c)
-        return (gate_ref[j, :, at].astype(f32) * cot_ref[j, :, at].astype(f32)).astype(bf16)
+        gate, cot = (gate_own, cot_own) if which is side else (gate_far, cot_far)
+        return (gate[c, j].astype(f32) * cot[c, j].astype(f32)).astype(bf16)
 
     def launch(c):
         x_copy(c).start()
-        for j in range(slots):
-            ws[c, j] = weigh(j, 1 - side, c)
+        load(0, far, c).wait()
+        load(1, far, c).wait()
+        for j in range(slots):
+            ws[c, j] = weigh(j, far, c)
         w_copy(c).start()
 
     def send_halo(c, part):
@@ -192,9 +234,12 @@
             cw[c, own + q] = gw[c, q]
 
     def gather_pair(c):
-        mine, theirs = side * slots, (1 - side) * slots
-        for j in range(slots):
-            cx[c, mine + j] = x_ref[j, :, lanes(side, c)]
+        mine, theirs = side * slots, far * slots
+        load_x(c).wait()
+        load(0, side, c).wait()
+        load(1, side, c).wait()
+        for j in range(slots):
+            cx[c, mine + j] = xo[c, j]
             cw[c, mine + j] = weigh(j, side, c)
         x_copy(c).wait_recv()
         w_copy(c).wait_recv()
@@ -239,18 +284,21 @@
             ao[u] = out[:, u * GROUP : (u + 1) * GROUP]
             vv[:, pl.ds(u * GROUP, GROUP)] = cw[c, tab[t_v + u]]
         for j in range(slots):
-            ig_ref[j, :, lanes(side, c)] = ao[tab[t_mine + j]].astype(bf16)
             sa[c, j] = ao[tab[t_theirs + j]].astype(bf16)
         a_copy(c).start()
+        for j in range(slots):
+            ig_own[c, j] = ao[tab[t_mine + j]].astype(bf16)
+        store(1, side, c).start()
         fill(cx, t_w, fmask_ref)
         out = jnp.dot(mat_a[...], rhs[...], preferred_element_type=f32)
         for u in range(own):
             co[u] = out[:, u * GROUP : (u + 1) * GROUP]
         for j in range(slots):
-            at = lanes(side, c)
-            gg_ref[j, :, at] = (cot_ref[j, :, at].astype(f32) * co[tab[t_mine + j]]).astype(bf16)
             sc[c, j] = co[tab[t_theirs + j]].astype(bf16)
         c_copy(c).start()
+        for j in range(slots):
+            conv_own[c, j] = co[tab[t_mine + j]].astype(bf16)
+        store(0, side, c).start()
         flip = (row + lane == rows - 1).astype(f32).astype(bf16)
         turned = jnp.dot(flip, vv[...], preferred_element_type=f32).astype(bf16)
         square = lax.dot_general(
@@ -269,13 +317,9 @@
 
     def finish(c):
         a_copy(c).wait_recv()
+        store(1, far, c).start()
         c_copy(c).wait_recv()
-        at = lanes(1 - side, c)
-        for j in range(slots):
-            ig_ref[j, :, at] = ra[c, j]
-            gg_ref[j, :, at] = (
-                cot_ref[j, :, at].astype(f32) * rc[c, j].astype(f32)
-            ).astype(bf16)
+        store(0, far, c).start()
 
     def over_ch(b, d, sender):
         start, size = batches[b]
@@ -398,10 +442,10 @@
         for u in range(own):
             for k in range(lags):
                 live = u < n
-                found = support_ref[jnp.clip(first + u, 0, total - 1), k] >= 0
+                found = support_ref[k, jnp.clip(first + u, 0, total - 1)] >= 0
                 put(fmask_ref, u * lags + lags - 1 - k, live & found)
                 later = first + u + k
-                found = support_ref[jnp.clip(later, 0, total - 1), k] >= 0
+                found = support_ref[k, jnp.clip(later, 0, total - 1)] >= 0
                 put(bmask_ref, u * lags + k, live & found & (later < total))
 
     for c in range(min(LEAD, chunks)):
@@ -452,6 +496,9 @@
 
     @pl.loop(0, chunks)
     def _(c):
+        for kind in range(2):
+            store(kind, side, c).wait()
+            store(kind, far, c).wait()
         x_copy(c).wait_send()
         w_copy(c).wait_send()
         a_copy(c).wait_send()
@@ -484,12 +531,20 @@
     vmem = pl.BlockSpec(memory_space=pltpu.VMEM)
     whole = jax.ShapeDtypeStruct(conv_input.shape, bf16)
     part = lambda count: pltpu.VMEM((chunks, count, rows, GROUP), bf16)
-    return pl.pallas_call(
+    hbm = pl.BlockSpec(memory_space=pl.ANY)
+    conv, input_grad, filter_grad = pl.pallas_call(
         functools.partial(kernel, n_ctx, n_ch, norm),
         out_shape=(whole, whole, jax.ShapeDtypeStruct(filters.shape, f32)),
-        in_specs=[pl.BlockSpec(memory_space=pltpu.SMEM)] * 2 + [vmem] * 4,
-        out_specs=(vmem, vmem, vmem),
+        in_specs=[pl.BlockSpec(memory_space=pltpu.SMEM)] * 2 + [hbm] * 3 + [vmem],
+        out_specs=(hbm, hbm, vmem),
         scratch_shapes=[
+            part(slots),
+            part(slots),
+            part(slots),
+            part(slots),
+            part(slots),
+            part(slots),
+            part(slots),
             part(slots),
             part(slots),
             part(slots),
@@ -525,6 +580,9 @@
             pltpu.SemaphoreType.DMA((2, n_ch)),
             pltpu.SemaphoreType.DMA((2, n_ctx)),
             pltpu.SemaphoreType.DMA((2, n_ctx)),
+            pltpu.SemaphoreType.DMA((2, 2, chunks)),
+            pltpu.SemaphoreType.DMA((chunks,)),
+            pltpu.SemaphoreType.DMA((2, 2, chunks)),
         ],
         compiler_params=pltpu.CompilerParams(
             collective_id=0, has_side_effects=True, vmem_limit_bytes=56 * 2**20
@@ -534,7 +592,9 @@
             bytes_accessed=10 * slots * rows * channels,
             transcendentals=0,
         ),
-    )(tile_owner, support, conv_input, gate_signal, cotangent, filters)
+    )(tile_owner, support.T, conv_input, gate_signal, cotangent, filters)
+    gate_grad = (cotangent.astype(f32) * conv.astype(f32)).astype(bf16)
+    return gate_grad, input_grad, filter_grad
 
 
 def solution(mesh):

time: 115 us -> 112 us (0.974)
  local copies, waits for them, and re-layouts: 6.62 us -> 1.96 us
  other arithmetic: 0 us -> 3.96 us
  Pallas kernels: 107 us -> 105 us
    unnamed x8, local copies, waits for them, and re-layouts: 6.62 us -> 1.96 us
    convert_element_type x0 -> x1, other arithmetic: none -> 3.96 us  [per_device(): gate_grad = (cotangent.astype(f32) * conv.astype(f32)).astype(bf16)]
    pallas_call x1, Pallas kernels: 107 us -> 105 us  [per_device(): pl.pallas_call(functools.partial(kernel, n_ctx, n_ch, norm), out_shape=(w...]
where the time goes in v3:
time: 112 us
  Pallas kernels  105 us (94%)
  other arithmetic  3.96 us (4%)
  local copies, waits for them, and re-layouts  1.96 us (2%)
    pallas_call x1, Pallas kernels, per_device(): pl.pallas_call(functools.partial(kernel, n_ctx, n_ch, norm), out_shape=(w...  105 us
    convert_element_type x1, other arithmetic, per_device(): gate_grad = (cotangent.astype(f32) * conv.astype(f32)).astype(bf16)  3.96 us

profile of v3, /device:TPU:0, one launch (start us, length us, event | category | flops | bytes accessed | tf_op | source)
XLA Modules:
  0.0 111.5 jit_solution(17710546350612504114)
XLA Ops:
  0.6 0.0 copy-start
  0.6 105.0 %shard_map.85 = (bf16[4,128,2048]{2,1,0:T(8,128)(2,1)}, bf16[4,128,2048]{2,1,0:T(8,128)(2,1)}, f32[16,1024]{1,0:T(8,128)}) custom-call(s32[24]{0:T(128)} %owner_ref.1, s32[8,24]{1,0:T(8,128)} %bitcast.1, bf16[4,128,2048]{2,1,0:T(8,128)(2,1)} %x_ref.1, bf16[4,128,2048]{2,1,0:T(8,128)(2,1)} %gate_ref.1, bf16[4,128,2048]{2,1,0:T(8,128)(2,1)} %cot_ref.1, ...), custom_call_target="tpu_custom_call" | custom-call | flops 6442450944 | bytes 10485760 | tf_op jit(solution)/shard_map/pallas_call | solution.py:535
  105.6 0.0 copy-done
  105.6 0.0 copy-start.1
  105.6 4.0 %multiply_convert_fusion = bf16[4,128,2048]{2,1,0:T(8,128)(2,1)} fusion(bf16[4,128,2048]{2,1,0:T(8,128)(2,1)} %get-tuple-element.6, bf16[4,128,2048]{2,1,0:T(8,128)(2,1)S(1)} %copy-done), kind=kLoop, calls=%fused_computation | loop fusion | flops 4194304 | bytes 6291456 | tf_op jit(solution)/shard_map/convert_element_type | solution.py:596
  109.6 0.0 copy-done.1
  109.6 0.0 copy-start.2
  109.6 1.3 %copy.11 = bf16[4,128,2048]{2,1,0:T(8,128)(2,1)} copy(bf16[4,128,2048]{2,1,0:T(8,128)(2,1)S(1)} %copy-done.1) | data formatting | bytes 4194304
  110.9 0.0 copy-done.2
  110.9 0.6 copy.12
Async XLA Ops:
  0.6 105.0 %copy-start = (bf16[4,128,2048]{2,1,0:T(8,128)(2,1)S(1)}, bf16[4,128,2048]{2,1,0:T(8,128)(2,1)}, u32[]{:S(2)}) copy-start(bf16[4,128,2048]{2,1,0:T(8,128)(2,1)} %cot_ref.1) | copy-start | bytes 6291460
  105.6 4.0 %copy-start.1 = (bf16[4,128,2048]{2,1,0:T(8,128)(2,1)S(1)}, bf16[4,128,2048]{2,1,0:T(8,128)(2,1)}, u32[]{:S(2)}) copy-start(bf16[4,128,2048]{2,1,0:T(8,128)(2,1)} %get-tuple-element.13) | copy-start | bytes 6291460
  109.6 1.3 %copy-start.2 = (f32[16,1024]{1,0:T(8,128)S(1)}, f32[16,1024]{1,0:T(8,128)}, u32[]{:S(2)}) copy-start(f32[16,1024]{1,0:T(8,128)} %get-tuple-element.14) | copy-start | bytes 196612

commit v4 on v3

--- a/solution.py
+++ b/solution.py
@@ -9,7 +9,7 @@
 from jax.sharding import PartitionSpec as P
 
 GROUP = 128
-LEAD = 2
+LEAD = 8
 LAG = 5
 LATE = 2
 LO = 4
@@ -37,7 +37,7 @@
     gate_ref,
     cot_ref,
     taps_ref,
-    conv_ref,
+    gg_ref,
     ig_ref,
     fg_ref,
     xo,
@@ -45,7 +45,8 @@
     gate_far,
     cot_own,
     cot_far,
-    conv_own,
+    gg_own,
+    gg_far,
     ig_own,
     xr,
     wr,
@@ -124,11 +125,11 @@
         return pltpu.make_async_copy(x_ref.at[:, :, lanes(side, c)], xo.at[c], x_sem.at[c])
 
     def store(kind, which, c):
-        dst = (conv_ref, ig_ref)[kind].at[:, :, lanes(which, c)]
+        dst = (gg_ref, ig_ref)[kind].at[:, :, lanes(which, c)]
         if which is side:
-            src = (conv_own, ig_own)[kind].at[c]
+            src = (gg_own, ig_own)[kind].at[c]
         else:
-            src = (rc, ra)[kind].at[c]
+            src = (gg_far, ra)[kind].at[c]
         at = 0 if which is side else 1
         return pltpu.make_async_copy(src, dst, out_sem.at[kind, at, c])
 
@@ -297,7 +298,7 @@
             sc[c, j] = co[tab[t_theirs + j]].astype(bf16)
         c_copy(c).start()
         for j in range(slots):
-            conv_own[c, j] = co[tab[t_mine + j]].astype(bf16)
+            gg_own[c, j] = (cot_own[c, j].astype(f32) * co[tab[t_mine + j]]).astype(bf16)
         store(0, side, c).start()
         flip = (row + lane == rows - 1).astype(f32).astype(bf16)
         turned = jnp.dot(flip, vv[...], preferred_element_type=f32).astype(bf16)
@@ -319,6 +320,8 @@
         a_copy(c).wait_recv()
         store(1, far, c).start()
         c_copy(c).wait_recv()
+        for j in range(slots):
+            gg_far[c, j] = (cot_far[c, j].astype(f32) * rc[c, j].astype(f32)).astype(bf16)
         store(0, far, c).start()
 
     def over_ch(b, d, sender):
@@ -480,11 +483,14 @@
             def _():
                 sum_over_ctx(b)
 
+        @pl.when(s == chunks + 3)
+        def _():
+            end_sums()
+
         @pl.when(s >= LAG)
         def _():
             finish(s - LAG)
 
-    end_sums()
     for b in range(2):
         @pl.loop(1, n_ch)
         def _(d):
@@ -513,6 +519,22 @@
         def _():
             w_down(c, 0).wait_send()
             w_down(c, 1).wait_send()
+
+
+def hand_over(slots, gg_in, ig_in, fg_in, gg_out, ig_out, fg_out, sem, fg_sem):
+    rows = gg_in.shape[1] // 2
+    copies = [pltpu.make_async_copy(fg_in, fg_out, fg_sem)]
+    for kind, (src, dst) in enumerate(((gg_in, gg_out), (ig_in, ig_out))):
+        for j in range(slots):
+            for part in range(2):
+                at = (j, pl.ds(part * rows, rows))
+                copies.append(
+                    pltpu.make_async_copy(src.at[at], dst.at[at], sem.at[kind, j, part])
+                )
+    for copy in copies:
+        copy.start()
+    for copy in copies:
+        copy.wait()
 
 
 def per_device(conv_input, gate_signal, cotangent, filters, tile_owner, support):
@@ -532,12 +554,13 @@
     whole = jax.ShapeDtypeStruct(conv_input.shape, bf16)
     part = lambda count: pltpu.VMEM((chunks, count, rows, GROUP), bf16)
     hbm = pl.BlockSpec(memory_space=pl.ANY)
-    conv, input_grad, filter_grad = pl.pallas_call(
+    results = pl.pallas_call(
         functools.partial(kernel, n_ctx, n_ch, norm),
         out_shape=(whole, whole, jax.ShapeDtypeStruct(filters.shape, f32)),
         in_specs=[pl.BlockSpec(memory_space=pltpu.SMEM)] * 2 + [hbm] * 3 + [vmem],
         out_specs=(hbm, hbm, vmem),
         scratch_shapes=[
+            part(slots),
             part(slots),
             part(slots),
             part(slots),
@@ -593,8 +616,17 @@
             transcendentals=0,
         ),
     )(tile_owner, support.T, conv_input, gate_signal, cotangent, filters)
-    gate_grad = (cotangent.astype(f32) * conv.astype(f32)).astype(bf16)
-    return gate_grad, input_grad, filter_grad
+    return pl.pallas_call(
+        functools.partial(hand_over, slots),
+        out_shape=(whole, whole, jax.ShapeDtypeStruct(filters.shape, f32)),
+        in_specs=[hbm] * 3,
+        out_specs=(hbm,) * 3,
+        scratch_shapes=[pltpu.SemaphoreType.DMA((2, slots, 2)), pltpu.SemaphoreType.DMA],
+        compiler_params=pltpu.CompilerParams(vmem_limit_bytes=60 * 2**20),
+        cost_estimate=pl.CostEstimate(
+            flops=0, bytes_accessed=8 * slots * rows * channels, transcendentals=0
+        ),
+    )(*results)
 
 
 def solution(mesh):

time: 112 us -> 236 us (2.11)
  Pallas kernels: 105 us -> 236 us
  other arithmetic: 3.96 us -> 0 us
    pallas_call x0 -> x1, Pallas kernels: none -> 130 us  [per_device(): pl.pallas_call(functools.partial(hand_over, slots), out_shape=(whole, who...]
    convert_element_type x1 -> x0, other arithmetic: 3.96 us -> none  [per_device(): gate_grad = (cotangent.astype(f32) * conv.astype(f32)).astype(bf16)]
where the time goes in v4:
time: 236 us
  Pallas kernels  236 us (100%)
    pallas_call x1, Pallas kernels, per_device(): pl.pallas_call(functools.partial(hand_over, slots), out_shape=(whole, who...  130 us
    pallas_call x1, Pallas kernels, per_device(): pl.pallas_call(functools.partial(kernel, n_ctx, n_ch, norm), out_shape=(w...  105 us

profile of v4, /device:TPU:0, one launch (start us, length us, event | category | flops | bytes accessed | tf_op | source)
XLA Modules:
  0.0 236.3 jit_solution(15950740658706177744)
XLA Ops:
  0.6 105.3 %shard_map.85 = (bf16[4,128,2048]{2,1,0:T(8,128)(2,1)}, bf16[4,128,2048]{2,1,0:T(8,128)(2,1)}, f32[16,1024]{1,0:T(8,128)}) custom-call(s32[24]{0:T(128)} %owner_ref.1, s32[8,24]{1,0:T(8,128)} %bitcast.1, bf16[4,128,2048]{2,1,0:T(8,128)(2,1)} %x_ref.1, bf16[4,128,2048]{2,1,0:T(8,128)(2,1)} %gate_ref.1, bf16[4,128,2048]{2,1,0:T(8,128)(2,1)} %cot_ref.1, ...), custom_call_target="tpu_custom_call" | custom-call | flops 6442450944 | bytes 10485760 | tf_op jit(solution)/shard_map/pallas_call | solution.py:557
  106.0 130.3 %shard_map.86 = (bf16[4,128,2048]{2,1,0:T(8,128)(2,1)}, bf16[4,128,2048]{2,1,0:T(8,128)(2,1)}, f32[16,1024]{1,0:T(8,128)}) custom-call(bf16[4,128,2048]{2,1,0:T(8,128)(2,1)} %get-tuple-element.6.gg_in, bf16[4,128,2048]{2,1,0:T(8,128)(2,1)} %get-tuple-element.7.ig_in, f32[16,1024]{1,0:T(8,128)} %get-tuple-element.8.fg_in), custom_call_target="tpu_custom_call" | custom-call | bytes 8388608 | tf_op jit(solution)/shard_map/pallas_call | solution.py:619

commit v5 on v4

--- a/solution.py
+++ b/solution.py
@@ -521,20 +521,24 @@
             w_down(c, 1).wait_send()
 
 
-def hand_over(slots, gg_in, ig_in, fg_in, gg_out, ig_out, fg_out, sem, fg_sem):
+def hand_over(slots, gg_in, ig_in, fg_in, gg_out, ig_out, fg_out, gg, ig, fg, sem, fg_sem):
     rows = gg_in.shape[1] // 2
-    copies = [pltpu.make_async_copy(fg_in, fg_out, fg_sem)]
-    for kind, (src, dst) in enumerate(((gg_in, gg_out), (ig_in, ig_out))):
-        for j in range(slots):
-            for part in range(2):
+    loads = [pltpu.make_async_copy(fg_in, fg, fg_sem.at[0])]
+    stores = [pltpu.make_async_copy(fg, fg_out, fg_sem.at[1])]
+    for j in range(slots):
+        for part in range(2):
+            for kind, (src, mid, dst) in enumerate(((gg_in, gg, gg_out), (ig_in, ig, ig_out))):
                 at = (j, pl.ds(part * rows, rows))
-                copies.append(
-                    pltpu.make_async_copy(src.at[at], dst.at[at], sem.at[kind, j, part])
-                )
-    for copy in copies:
-        copy.start()
-    for copy in copies:
-        copy.wait()
+                sems = sem.at[0, kind, j, part], sem.at[1, kind, j, part]
+                loads.append(pltpu.make_async_copy(src.at[at], mid.at[at], sems[0]))
+                stores.append(pltpu.make_async_copy(mid.at[at], dst.at[at], sems[1]))
+    for load in loads:
+        load.start()
+    for load, store in zip(loads, stores):
+        load.wait()
+        store.start()
+    for store in stores:
+        store.wait()
 
 
 def per_device(conv_input, gate_signal, cotangent, filters, tile_owner, support):
@@ -621,7 +625,13 @@
         out_shape=(whole, whole, jax.ShapeDtypeStruct(filters.shape, f32)),
         in_specs=[hbm] * 3,
         out_specs=(hbm,) * 3,
-        scratch_shapes=[pltpu.SemaphoreType.DMA((2, slots, 2)), pltpu.SemaphoreType.DMA],
+        scratch_shapes=[
+            pltpu.VMEM(conv_input.shape, bf16),
+            pltpu.VMEM(conv_input.shape, bf16),
+            pltpu.VMEM(filters.shape, f32),
+            pltpu.SemaphoreType.DMA((2, 2, slots, 2)),
+            pltpu.SemaphoreType.DMA((2,)),
+        ],
         compiler_params=pltpu.CompilerParams(vmem_limit_bytes=60 * 2**20),
         cost_estimate=pl.CostEstimate(
             flops=0, bytes_accessed=8 * slots * rows * channels, transcendentals=0

time: 236 us -> 110 us (0.47)
  Pallas kernels: 236 us -> 110 us
    pallas_call x1, Pallas kernels: 130 us -> 4.33 us  [per_device(): pl.pallas_call(functools.partial(hand_over, slots), out_shape=(whole, who...]
where the time goes in v5:
time: 110 us
  Pallas kernels  110 us (100%)
    pallas_call x1, Pallas kernels, per_device(): pl.pallas_call(functools.partial(kernel, n_ctx, n_ch, norm), out_shape=(w...  105 us
    pallas_call x1, Pallas kernels, per_device(): pl.pallas_call(functools.partial(hand_over, slots), out_shape=(whole, who...  4.33 us

profile of v5, /device:TPU:0, one launch (start us, length us, event | category | flops | bytes accessed | tf_op | source)
XLA Modules:
  0.0 110.3 jit_solution(8996916677501073703)
XLA Ops:
  0.6 105.3 %shard_map.85 = (bf16[4,128,2048]{2,1,0:T(8,128)(2,1)}, bf16[4,128,2048]{2,1,0:T(8,128)(2,1)}, f32[16,1024]{1,0:T(8,128)}) custom-call(s32[24]{0:T(128)} %owner_ref.1, s32[8,24]{1,0:T(8,128)} %bitcast.1, bf16[4,128,2048]{2,1,0:T(8,128)(2,1)} %x_ref.1, bf16[4,128,2048]{2,1,0:T(8,128)(2,1)} %gate_ref.1, bf16[4,128,2048]{2,1,0:T(8,128)(2,1)} %cot_ref.1, ...), custom_call_target="tpu_custom_call" | custom-call | flops 6442450944 | bytes 10485760 | tf_op jit(solution)/shard_map/pallas_call | solution.py:561
  106.0 4.3 %shard_map.86 = (bf16[4,128,2048]{2,1,0:T(8,128)(2,1)}, bf16[4,128,2048]{2,1,0:T(8,128)(2,1)}, f32[16,1024]{1,0:T(8,128)}) custom-call(bf16[4,128,2048]{2,1,0:T(8,128)(2,1)} %get-tuple-element.6.gg_in, bf16[4,128,2048]{2,1,0:T(8,128)(2,1)} %get-tuple-element.7.ig_in, f32[16,1024]{1,0:T(8,128)} %get-tuple-element.8.fg_in), custom_call_target="tpu_custom_call" | custom-call | bytes 8388608 | tf_op jit(solution)/shard_map/pallas_call | solution.py:623

commit v6 on v5

--- a/solution.py
+++ b/solution.py
@@ -41,6 +41,7 @@
     ig_ref,
     fg_ref,
     xo,
+    xf,
     gate_own,
     gate_far,
     cot_own,
@@ -122,7 +123,10 @@
         )
 
     def load_x(c):
-        return pltpu.make_async_copy(x_ref.at[:, :, lanes(side, c)], xo.at[c], x_sem.at[c])
+        return pltpu.make_async_copy(x_ref.at[:, :, lanes(side, c)], xo.at[c], x_sem.at[0, c])
+
+    def load_far_x(c):
+        return pltpu.make_async_copy(x_ref.at[:, :, lanes(far, c)], xf.at[c], x_sem.at[1, c])
 
     def store(kind, which, c):
         dst = (gg_ref, ig_ref)[kind].at[:, :, lanes(which, c)]
@@ -137,6 +141,7 @@
 
     @pl.loop(0, chunks)
     def _(c):
+        load_far_x(c).start()
         load(0, far, c).start()
         load(1, far, c).start()
         load_x(c).start()
@@ -172,7 +177,7 @@
 
     def x_copy(c):
         return copy_to(
-            x_ref.at[:, :, lanes(far, c)], xr.at[c], y_send.at[0, c], y_recv.at[0, c], partner
+            xf.at[c], xr.at[c], y_send.at[0, c], y_recv.at[0, c], partner
         )
 
     def w_copy(c):
@@ -201,6 +206,7 @@
         return (gate[c, j].astype(f32) * cot[c, j].astype(f32)).astype(bf16)
 
     def launch(c):
+        load_far_x(c).wait()
         x_copy(c).start()
         load(0, far, c).wait()
         load(1, far, c).wait()
@@ -564,6 +570,7 @@
         in_specs=[pl.BlockSpec(memory_space=pltpu.SMEM)] * 2 + [hbm] * 3 + [vmem],
         out_specs=(hbm, hbm, vmem),
         scratch_shapes=[
+            part(slots),
             part(slots),
             part(slots),
             part(slots),
@@ -608,7 +615,7 @@
             pltpu.SemaphoreType.DMA((2, n_ctx)),
             pltpu.SemaphoreType.DMA((2, n_ctx)),
             pltpu.SemaphoreType.DMA((2, 2, chunks)),
-            pltpu.SemaphoreType.DMA((chunks,)),
+            pltpu.SemaphoreType.DMA((2, chunks)),
             pltpu.SemaphoreType.DMA((2, 2, chunks)),
         ],
         compiler_params=pltpu.CompilerParams(

time: 110 us -> 110 us (level)
  no operation moved by 1% of the time
where the time goes in v6:
time: 110 us
  Pallas kernels  110 us (100%)
    pallas_call x1, Pallas kernels, per_device(): pl.pallas_call(functools.partial(kernel, n_ctx, n_ch, norm), out_shape=(w...  105 us
    pallas_call x1, Pallas kernels, per_device(): pl.pallas_call(functools.partial(hand_over, slots), out_shape=(whole, who...  4.33 us

profile of v6, /device:TPU:0, one launch (start us, length us, event | category | flops | bytes accessed | tf_op | source)
XLA Modules:
  0.0 110.2 jit_solution(805821266262603677)
XLA Ops:
  0.6 105.2 %shard_map.85 = (bf16[4,128,2048]{2,1,0:T(8,128)(2,1)}, bf16[4,128,2048]{2,1,0:T(8,128)(2,1)}, f32[16,1024]{1,0:T(8,128)}) custom-call(s32[24]{0:T(128)} %owner_ref.1, s32[8,24]{1,0:T(8,128)} %bitcast.1, bf16[4,128,2048]{2,1,0:T(8,128)(2,1)} %x_ref.1, bf16[4,128,2048]{2,1,0:T(8,128)(2,1)} %gate_ref.1, bf16[4,128,2048]{2,1,0:T(8,128)(2,1)} %cot_ref.1, ...), custom_call_target="tpu_custom_call" | custom-call | flops 6442450944 | bytes 10485760 | tf_op jit(solution)/shard_map/pallas_call | solution.py:567
  105.9 4.3 %shard_map.86 = (bf16[4,128,2048]{2,1,0:T(8,128)(2,1)}, bf16[4,128,2048]{2,1,0:T(8,128)(2,1)}, f32[16,1024]{1,0:T(8,128)}) custom-call(bf16[4,128,2048]{2,1,0:T(8,128)(2,1)} %get-tuple-element.6.gg_in, bf16[4,128,2048]{2,1,0:T(8,128)(2,1)} %get-tuple-element.7.ig_in, f32[16,1024]{1,0:T(8,128)} %get-tuple-element.8.fg_in), custom_call_target="tpu_custom_call" | custom-call | bytes 8388608 | tf_op jit(solution)/shard_map/pallas_call | solution.py:630
